TPU v7x, 128 devices: a whole 4x4x4 slice. The times are simulated.
128 devices in a mesh: gx: 8 (over z, core), gy: 16 (over x, y).
Axes of the slice: x: 4, y: 4, z: 4, core: 2. Of those that a mesh axis runs over, the one named last changes fastest.
Arguments:
- field: float32 [32, 4096, 4096], P(None, 'gx', 'gy'), may hold values from -6 to 6
- mode2_factor: float32 [4096, 64], P('gy'), may hold values from -0.09375 to 0.09375
- mode3_factor: float32 [32, 16], replicated, may hold values from -1 to 1
- start_factor: float32 [4096, 64], P('gx'), may hold values from -0.09375 to 0.09375
Outputs:
- new_factor: float32 [4096, 64], P('gx')
All inputs are finite; a program needn't handle non-finite values.
Results may differ from a plain program's by a relative error of at most 0.0003.
Values sent between devices are 32-bit elements; how exact they have to be, the bound alone decides.
A program may use at most 64 MiB of HBM per device.

v0:
```python
import jax
import jax.numpy as jnp
from jax import lax
from jax.sharding import PartitionSpec as P

ITERS = 2


HIGH = lax.Precision.HIGHEST


def solve_right(lower, matrix):
    return lax.linalg.triangular_solve(lower, matrix, left_side=False, lower=True, transpose_a=True)


def left_columns(unfolded_t, basis):
    return lax.psum(jnp.dot(unfolded_t, basis, precision=HIGH), "gx")


def image_columns(unfolded_t, left):
    return lax.psum(
        lax.dot_general(unfolded_t, left, (((0,), (0,)), ((), ())), precision=HIGH), "gy"
    )


def on_device(field, mode2_factor, mode3_factor, start_factor):
    local_rows = field.shape[1]
    rank_two = mode2_factor.shape[1]
    rank_three = mode3_factor.shape[1]
    total_rows = local_rows * lax.axis_size("gx")
    timed = jnp.einsum("tab,ts->sab", field, mode3_factor, precision=HIGH)
    pair_rows = rank_two * rank_three // lax.axis_size("gy")
    part = jnp.einsum("sab,bq->qsa", timed, mode2_factor, precision=HIGH)
    unfolded_t = lax.psum_scatter(
        part.reshape(lax.axis_size("gy") * pair_rows, local_rows),
        "gy",
        scatter_dimension=0,
        tiled=True,
    )
    basis = start_factor
    for step in range(ITERS):
        left = left_columns(unfolded_t, basis)
        image = image_columns(unfolded_t, left)
        gram = lax.psum(jnp.dot(image.T, image, precision=HIGH), "gx")
        lower = jnp.linalg.cholesky(gram)
        basis = solve_right(lower, image)
    return basis * jnp.sqrt(jnp.float32(total_rows))


def solution(mesh):
    placed = (P(None, "gx", "gy"), P("gy", None), P(), P("gx", None))
    return jax.shard_map(
        on_device, mesh=mesh, in_specs=placed, out_specs=P("gx", None), check_vma=False
    )
```

profile of v0, /device:TPU:1, one launch (start us, length us, event | category | flops | bytes accessed | tf_op | source)
XLA Modules:
  0.0 410.4 jit_solution(14912413954015969464)
XLA Ops:
  6.5 19.9 %fusion = f32[16,512,256]{2,0,1:T(8,128)S(1)} fusion(f32[32,512,256]{2,1,0:T(8,128)} %param.7, f32[32,16]{0,1:T(8,128)} %param.9), kind=kOutput, calls=%fused_computation | convolution fusion | flops 805306368 | bytes 25167872 | tf_op jit(solution)/shard_map/tab,ts->sab/dot_general | solution.py:31
  26.5 8.2 %convolution_bitcast_fusion = f32[64,16,512]{0,1,2:T(8,128)} fusion(f32[16,512,256]{2,0,1:T(8,128)S(1)} %fusion, f32[256,64]{0,1:T(8,128)S(1)} %copy-done.1), kind=kOutput, calls=%fused_computation.2 | convolution fusion | flops 1610612736 | bytes 10551296 | tf_op jit(solution)/shard_map/sab,bq->qsa/dot_general | solution.py:33
  34.7 4.5 %copy.9 = f32[64,16,512]{2,1,0:T(8,128)} copy(f32[64,16,512]{0,1,2:T(8,128)} %convolution_bitcast_fusion) | data formatting | bytes 4194304 | tf_op jit(solution)/shard_map/sab,bq->qsa/dot_general | solution.py:33
  39.3 75.8 %reduce-scatter.2.cloned.1.call-done = f32[64,512]{1,0:T(8,128)} async-done(((f32[1024,512]{1,0:T(8,128)}), f32[64,512]{1,0:T(8,128)}) %reduce-scatter.2.cloned.1.call-update) | async-done | bytes 131088 | tf_op jit(solution)/shard_map/reduce_scatter | solution.py:34
  115.1 1.2 fusion.13
  116.3 23.0 %psum.42 = f32[64,64]{1,0:T(8,128)S(1)} all-reduce(f32[64,64]{1,0:T(8,128)S(1)} %fusion.13), channel_id=1, replica_groups=mesh['gx'=8,'gy'=16] {'gx'}, use_global_device_ids=true, to_apply=%region_1.0 | all-reduce | flops 4096 | bytes 32768 | tf_op jit(solution)/shard_map/psum | solution.py:17
  139.3 1.9 fusion.14
  141.2 80.0 %all-reduce.3.cloned.1.call-done = f32[512,64]{0,1:T(8,128)} async-done(((f32[512,64]{0,1:T(8,128)}), f32[512,64]{0,1:T(8,128)}) %all-reduce.3.cloned.1.call-update) | async-done | bytes 131088 | tf_op jit(solution)/shard_map/psum | solution.py:21
  221.2 1.2 fusion.15
  222.4 23.0 %psum.44 = f32[64,64]{0,1:T(8,128)S(1)} all-reduce(f32[64,64]{0,1:T(8,128)S(1)} %fusion.15), channel_id=1, replica_groups=mesh['gx'=8,'gy'=16] {'gx'}, use_global_device_ids=true, to_apply=%region_3.0 | all-reduce | flops 4096 | bytes 32768 | tf_op jit(solution)/shard_map/psum | solution.py:44
  245.5 5.8 %cholesky.44 = f32[64,64]{1,0:T(8,128)S(1)} custom-call(f32[64,64]{1,0:T(8,128)S(1)} %fusion.9), custom_call_target="Cholesky" | custom-call | tf_op jit(solution)/shard_map/jit(cholesky)/cholesky | solution.py:45
  252.1 0.7 fusion.4
  252.7 4.9 %custom-call.6 = f32[1,64,64]{1,2,0:T(8,128)S(1)} custom-call(f32[1,64,64]{2,1,0:T(8,128)S(1)} %fusion.4), custom_call_target="InvertDiagBlocksLowerTriangular" | custom-call | tf_op jit(solution)/shard_map/triangular_solve/custom-call.0 | solution.py:13
  257.6 1.2 convolution_bitcast_fusion.2
  258.9 1.2 fusion.16
  260.0 23.6 %psum.45 = f32[64,64]{1,0:T(8,128)S(1)} all-reduce(f32[64,64]{1,0:T(8,128)S(1)} %fusion.16), channel_id=1, replica_groups=mesh['gx'=8,'gy'=16] {'gx'}, use_global_device_ids=true, to_apply=%region_6.9 | all-reduce | flops 4096 | bytes 32768 | tf_op jit(solution)/shard_map/psum | solution.py:17
  283.6 1.9 fusion.17
  285.5 80.1 %all-reduce.5.cloned.1.call-done = f32[512,64]{0,1:T(8,128)} async-done(((f32[512,64]{0,1:T(8,128)}), f32[512,64]{0,1:T(8,128)}) %all-reduce.5.cloned.1.call-update) | async-done | bytes 131088 | tf_op jit(solution)/shard_map/psum | solution.py:21
  365.6 1.2 fusion.18
  366.9 22.9 %psum.47 = f32[64,64]{0,1:T(8,128)S(1)} all-reduce(f32[64,64]{0,1:T(8,128)S(1)} %fusion.18), channel_id=1, replica_groups=mesh['gx'=8,'gy'=16] {'gx'}, use_global_device_ids=true, to_apply=%region_8.11 | all-reduce | flops 4096 | bytes 32768 | tf_op jit(solution)/shard_map/psum | solution.py:44
  389.9 5.8 %cholesky.55 = f32[64,64]{1,0:T(8,128)S(1)} custom-call(f32[64,64]{1,0:T(8,128)S(1)} %fusion.7), custom_call_target="Cholesky" | custom-call | tf_op jit(solution)/shard_map/jit(cholesky)/cholesky | solution.py:45
  396.4 0.7 fusion.5
  397.1 4.9 %custom-call.7 = f32[1,64,64]{1,2,0:T(8,128)S(1)} custom-call(f32[1,64,64]{2,1,0:T(8,128)S(1)} %fusion.5), custom_call_target="InvertDiagBlocksLowerTriangular" | custom-call | tf_op jit(solution)/shard_map/triangular_solve/custom-call.0 | solution.py:13
  402.0 1.9 fusion.2
  (18 shorter events, 1.7 us)
Async XLA Ops:
  6.5 108.6 %copy-start = (f32[512,64]{0,1:T(8,128)S(1)}, f32[512,64]{0,1:T(8,128)}, u32[]{:S(2)}) copy-start(f32[512,64]{0,1:T(8,128)} %param.10) | copy-start | bytes 393220
  6.5 19.9 %copy-start.1 = (f32[256,64]{0,1:T(8,128)S(1)}, f32[256,64]{0,1:T(8,128)}, u32[]{:S(2)}) copy-start(f32[256,64]{0,1:T(8,128)} %param.8) | copy-start | bytes 196612
  6.5 108.6 %reduce-scatter.2.cloned.1.call-start = ((), (), s32[]{:S(2)}) async-start(), calls=%async_computation.1 | async-start | bytes 2228224 | tf_op jit(solution)/shard_map/reduce_scatter | solution.py:34
  39.3 181.9 %all-reduce.3.cloned.1.call-start = ((), (), s32[]{:S(2)}) async-start(), calls=%async_computation.2 | async-start | bytes 262144 | tf_op jit(solution)/shard_map/psum | solution.py:21
  141.2 224.5 %all-reduce.5.cloned.1.call-start = ((), (), s32[]{:S(2)}) async-start(), calls=%async_computation.3 | async-start | bytes 262144 | tf_op jit(solution)/shard_map/psum | solution.py:21
Sparse Core Ops, SparseCore 0:
  39.4 75.7 reduce-scatter.1
  141.3 79.8 all-reduce.2
  285.6 79.9 all-reduce.4
where the time goes:
time: 413 us; the launch traced here: 410 us
  waiting for transfers between devices  236 us (57%)
  blocking collectives  92.5 us (22%)
  matrix products  39.8 us (10%)
  other arithmetic  24.2 us (6%)
  between operations  13.2 us (3%)
  local copies, waits for them, and re-layouts  4.69 us (1%)
    psum x2, waiting for transfers between devices, image_columns(): lax.psum(lax.dot_general(unfolded_t, left, (((0,), (0,)), ((), ())), prec...  160 us
    reduce_scatter x1, waiting for transfers between devices, on_device(): lax.psum_scatter(part.reshape(lax.axis_size('gy') * pair_rows, local_rows...  75.8 us
    psum x2, blocking collectives, left_columns(): return lax.psum(jnp.dot(unfolded_t, basis, precision=HIGH), 'gx')  46.6 us
    psum x2, blocking collectives, on_device(): gram = lax.psum(jnp.dot(image.T, image, precision=HIGH), 'gx')  45.9 us
    dot_general x1, matrix products, on_device(): timed = jnp.einsum('tab,ts->sab', field, mode3_factor, precision=HIGH)  19.9 us
    another operation x6, other arithmetic, on_device(): lower = jnp.linalg.cholesky(gram)  13 us
    another operation x4, other arithmetic, solve_right(): lax.linalg.triangular_solve(lower, matrix, left_side=False, lower=True, t...  11.1 us
  transfers between devices with their start and end apart: 3, of which 3 were waited for; matrix products, arithmetic and copies ran while one was open for 0% of the time, Pallas kernels for 0%

commit v1 on v0

v1 whole, which is shorter than its diff:
```python
import jax
import jax.numpy as jnp
from jax import lax
from jax.experimental import pallas as pl
from jax.experimental.pallas import tpu as pltpu
from jax.sharding import PartitionSpec as P

MESH = pl.DeviceIdType.MESH
HIGH = lax.Precision.HIGHEST
F32 = jnp.float32
BF16 = jnp.bfloat16

T3 = 32
R3 = 16
RANK = 64
ROWS = 512
COLS = 256
GX = 8
GY = 16
CHUNKS = 8
CHUNK = ROWS // CHUNKS
PACKED = ROWS // 2
SHARE = PACKED // GY
NN = (((1,), (0,)), ((), ()))
NT = (((1,), (1,)), ((), ()))
TN = (((0,), (0,)), ((), ()))


def dot(a, b, dims=NN):
    return lax.dot_general(a, b, dims, precision=HIGH, preferred_element_type=F32)


def bdot(a, b):
    return lax.dot_general(a, b, NN, preferred_element_type=F32)


def split(a):
    high = a.astype(BF16)
    return high, (a - high.astype(F32)).astype(BF16)


def swap(a):
    return pltpu.roll(a, 64, 1)


def lower_lanes(shape):
    return lax.broadcasted_iota(jnp.int32, shape, 1) < 64


def fold(m):
    return m[:64] + swap(m[64:])


def pair_up(s):
    return jnp.where(lower_lanes((32, 128)), s[:32], swap(s[32:]))


def unpair(p):
    return jnp.concatenate([p, swap(p)], axis=0)


def twice(s):
    low = lower_lanes((64, 128))
    zero = jnp.zeros_like(s)
    return jnp.concatenate([jnp.where(low, s, zero), jnp.where(low, zero, swap(s))], axis=0)


def inverse_factor(gram):
    lane = lax.broadcasted_iota(jnp.int32, (8, 128), 1)
    row = lax.broadcasted_iota(jnp.int32, (8, 128), 0)
    tiles = []
    for b in range(8):
        unit = jnp.where(lane == row + (64 + 8 * b), 1.0, 0.0)
        tiles.append(jnp.where(lane < 64, gram[8 * b : 8 * b + 8], unit))
    for k in range(64):
        own, at = divmod(k, 8)
        line = tiles[own][at : at + 1]
        scaled = line * (1.0 / line[:, k : k + 1])
        for b in range(own, 8):
            col = tiles[b][:, k : k + 1]
            if b == own:
                col = jnp.where(row[:, :1] > at, col, 0.0)
            tiles[b] = tiles[b] - col * scaled
    out = []
    for b in range(8):
        diag = jnp.sum(jnp.where(lane == row + 8 * b, tiles[b], 0.0), axis=1, keepdims=True)
        out.append(tiles[b] * lax.rsqrt(diag))
    return swap(jnp.concatenate(out, axis=0))


def kernel(
    field_hbm, m2_hbm, m3_hbm, start_hbm, out_ref,
    field, m2, m3, start,
    part, got, pair, basis, left_out, left_in, image, share_in, share, full,
    in_sem, small_sem, rs_send, rs_recv, x_send, x_recv, s_send, s_recv, g_send, g_recv,
):
    mx = lax.axis_index("gx")
    my = lax.axis_index("gy")

    small = [
        pltpu.make_async_copy(src, dst, small_sem.at[n])
        for n, (src, dst) in enumerate(((m2_hbm, m2), (m3_hbm, m3), (start_hbm, start)))
    ]
    loads = [
        pltpu.make_async_copy(
            field_hbm.at[:, pl.ds(c * CHUNK, CHUNK), :],
            field.at[:, pl.ds(c * CHUNK, CHUNK), :],
            in_sem.at[c],
        )
        for c in range(CHUNKS)
    ]
    small[0].start()
    small[1].start()
    for copy in loads:
        copy.start()
    small[2].start()

    barrier = pltpu.get_barrier_semaphore()

    @pl.loop(1, GY)
    def _(r):
        pl.semaphore_signal(barrier, inc=1, device_id={"gy": lax.rem(my + r, GY)}, device_id_type=MESH)

    @pl.loop(1, GX)
    def _(r):
        pl.semaphore_signal(barrier, inc=1, device_id={"gx": lax.rem(mx + r, GX)}, device_id_type=MESH)

    small[0].wait()
    small[1].wait()
    m2h, m2l = split(m2[...])
    right = jnp.concatenate([m2h, m2l], axis=1)
    tall = jnp.where(
        lax.broadcasted_iota(jnp.int32, (128, R3), 0) // 8 == lax.broadcasted_iota(jnp.int32, (128, R3), 1), 1.0, 0.0
    )
    wide = jnp.where(
        lax.broadcasted_iota(jnp.int32, (T3, 256), 0) == lax.broadcasted_iota(jnp.int32, (T3, 256), 1) // 8, 1.0, 0.0
    )
    spread = dot(dot(tall, m3[...], NT), wide)
    same = (
        lax.broadcasted_iota(jnp.int32, (128, 256), 0) % 8 == lax.broadcasted_iota(jnp.int32, (128, 256), 1) % 8
    )
    wh, wl = split(jnp.where(same, spread, 0.0))
    w2 = jnp.concatenate([wh, wl], axis=0)
    low = lower_lanes((128, 128))

    def project(i0):
        tile = field[:, pl.ds(i0, 8), :].reshape(T3 * 8, COLS)
        th, tl = split(tile)
        return bdot(th, right) + bdot(tl, right)

    for c in range(CHUNKS):
        loads[c].wait()

        @pl.loop(0, CHUNK // 16)
        def _(n):
            i0 = pl.multiple_of(c * CHUNK + n * 16, 16)
            both = jnp.concatenate([project(i0), project(i0 + 8)], axis=1)
            bh, bl = split(both)
            two = bdot(w2, bh)
            res = two[:128] + two[128:] + bdot(wh, bl)
            a, b = res[:, :128], res[:, 128:]
            done = jnp.where(low, a + swap(a), b + swap(b))
            part[:, pl.ds(pl.multiple_of(i0 // 2, 8), 8), :] = done.reshape(R3, 8, 128)

        if c == 0:
            pl.semaphore_wait(barrier, GX + GY - 2)

        @pl.loop(1, GY)
        def _(r):
            dest = lax.rem(my + r, GY)
            at = pl.ds(c * (CHUNK // 2), CHUNK // 2)
            pltpu.make_async_remote_copy(
                part.at[dest, at], got.at[r - 1, at], rs_send, rs_recv,
                device_id={"gy": dest}, device_id_type=MESH,
            ).start()

    small[2].wait()
    halves = start[...].reshape(ROWS // 16, 2, 8, RANK)
    basis[...] = jnp.concatenate([halves[:, 0], halves[:, 1]], axis=2).reshape(PACKED, 128)

    pltpu.make_async_copy(got, got, rs_recv).wait()
    own = part[my]
    for r in range(GY - 1):
        own = own + got[r]
    pair[...] = own
    pltpu.make_async_copy(got, got, rs_send).wait()

    def sum_over_gx(n, rows, value):
        src = left_out.at[n, pl.ds(0, rows)]
        dst = left_in.at[n, :, pl.ds(0, rows)]
        src[...] = value

        @pl.loop(1, GX)
        def _(r):
            pltpu.make_async_remote_copy(
                src, left_in.at[n, r - 1, pl.ds(0, rows)], x_send.at[n], x_recv.at[n],
                device_id={"gx": lax.rem(mx + r, GX)}, device_id_type=MESH,
            ).start()

        pltpu.make_async_copy(dst, dst, x_recv.at[n]).wait()
        total = value
        for r in range(GX - 1):
            total = total + left_in[n, r, :rows]
        return total, lambda: pltpu.make_async_copy(dst, dst, x_send.at[n]).wait()

    def sum_over_gy(n, value, beside):
        image[n] = value

        @pl.loop(1, GY)
        def _(r):
            dest = lax.rem(my + r, GY)
            pltpu.make_async_remote_copy(
                image.at[n, pl.ds(pl.multiple_of(dest * SHARE, SHARE), SHARE)], share_in.at[n, r - 1],
                s_send.at[n], s_recv.at[n], device_id={"gy": dest}, device_id_type=MESH,
            ).start()

        pltpu.make_async_copy(share_in.at[n], share_in.at[n], s_recv.at[n]).wait()
        total = image[n, pl.ds(pl.multiple_of(my * SHARE, SHARE), SHARE)]
        for r in range(GY - 1):
            total = total + share_in[n, r]
        share[n] = total
        full[n, my] = total

        @pl.loop(1, GY)
        def _(r):
            pltpu.make_async_remote_copy(
                share.at[n], full.at[n, my], g_send.at[n], g_recv.at[n],
                device_id={"gy": lax.rem(my + r, GY)}, device_id_type=MESH,
            ).start()

        aside = beside()
        pltpu.make_async_copy(share_in.at[n], share_in.at[n], g_recv.at[n]).wait()

        def end():
            pltpu.make_async_copy(share_in.at[n], share_in.at[n], s_send.at[n]).wait()
            pltpu.make_async_copy(share_in.at[n], share_in.at[n], g_send.at[n]).wait()

        return full[n].reshape(PACKED, 128), aside, end

    low64 = lower_lanes((64, 128))
    total, end0 = sum_over_gx(0, 32, pair_up(fold(dot(pair[...], basis[...], TN))))
    image1, _, end1 = sum_over_gy(0, dot(pair[...], twice(unpair(total))), lambda: None)
    left = fold(dot(pair[...], image1, TN))
    gram = fold(dot(image1, image1, TN))
    total, end2 = sum_over_gx(1, 64, jnp.where(low64, left, swap(gram)))
    raw, factor, end3 = sum_over_gy(
        1, dot(pair[...], twice(total)), lambda: inverse_factor(swap(total))
    )
    image2 = dot(raw, twice(factor), NT)
    gram = fold(dot(image2, image2, TN))
    total, end4 = sum_over_gx(2, 32, pair_up(gram))
    factor = inverse_factor(unpair(total))
    final = dot(image2, twice(factor), NT) * jnp.sqrt(F32(ROWS * GX))
    final = final.reshape(ROWS // 16, 8, 128)
    for h in range(2):
        out_ref[:, h] = final[:, :, 64 * h : 64 * h + 64]
    for end in (end0, end1, end2, end3, end4):
        end()


def on_device(field, mode2_factor, mode3_factor, start_factor):
    dma = pltpu.SemaphoreType.DMA
    out = pl.pallas_call(
        kernel,
        out_shape=jax.ShapeDtypeStruct((ROWS // 16, 2, 8, RANK), F32),
        in_specs=[pl.BlockSpec(memory_space=pl.ANY)] * 4,
        out_specs=pl.BlockSpec(memory_space=pltpu.VMEM),
        scratch_shapes=[
            pltpu.VMEM((T3, ROWS, COLS), F32),
            pltpu.VMEM((COLS, RANK), F32),
            pltpu.VMEM((T3, R3), F32),
            pltpu.VMEM((ROWS, RANK), F32),
            pltpu.VMEM((R3, PACKED, 128), F32),
            pltpu.VMEM((GY - 1, PACKED, 128), F32),
            pltpu.VMEM((PACKED, 128), F32),
            pltpu.VMEM((PACKED, 128), F32),
            pltpu.VMEM((3, 64, 128), F32),
            pltpu.VMEM((3, GX - 1, 64, 128), F32),
            pltpu.VMEM((2, PACKED, 128), F32),
            pltpu.VMEM((2, GY - 1, SHARE, 128), F32),
            pltpu.VMEM((2, SHARE, 128), F32),
            pltpu.VMEM((2, GY, SHARE, 128), F32),
            dma((CHUNKS,)),
            dma((3,)),
            dma, dma,
            dma((3,)), dma((3,)),
            dma((2,)), dma((2,)),
            dma((2,)), dma((2,)),
        ],
        compiler_params=pltpu.CompilerParams(
            collective_id=0, has_side_effects=True, vmem_limit_bytes=48 * 1024 * 1024
        ),
    )(field, mode2_factor, mode3_factor, start_factor)
    return out.reshape(ROWS, RANK)


def solution(mesh):
    placed = (P(None, "gx", "gy"), P("gy", None), P(), P("gx", None))
    return jax.shard_map(
        on_device, mesh=mesh, in_specs=placed, out_specs=P("gx", None), check_vma=False
    )
```

time: 413 us -> 81.6 us (0.20)
  waiting for transfers between devices: 236 us -> 0 us
  blocking collectives: 92.5 us -> 0 us
  Pallas kernels: 0 us -> 77.9 us
  matrix products: 39.8 us -> 0 us
  other arithmetic: 24.2 us -> 0 us
  between operations: 13.2 us -> 0.02 us
    psum x2 -> x0, waiting for transfers between devices: 160 us -> none  [image_columns(): lax.psum(lax.dot_general(unfolded_t, left, (((0,), (0,)), ((), ())), prec...]
    psum x4 -> x0, blocking collectives: 92.5 us -> none  [the longest x2 46.6 us: left_columns(): return lax.psum(jnp.dot(unfolded_t, basis, precision=HIGH), 'gx')]
    pallas_call x0 -> x1, Pallas kernels: none -> 77.9 us  [on_device(): pl.pallas_call(kernel, out_shape=jax.ShapeDtypeStruct((ROWS // 16, 2, 8,...]
    reduce_scatter x1 -> x0, waiting for transfers between devices: 75.8 us -> none  [on_device(): lax.psum_scatter(part.reshape(lax.axis_size('gy') * pair_rows, local_rows...]
    dot_general x8 -> x0, matrix products: 36.7 us -> none  [the longest x1 19.9 us: on_device(): timed = jnp.einsum('tab,ts->sab', field, mode3_factor, precision=HIGH)]
    another operation x10 -> x0, other arithmetic: 24.1 us -> none  [the longest x6 13 us: on_device(): lower = jnp.linalg.cholesky(gram)]
    dot_general x1 -> x0, local copies, waits for them, and re-layouts: 4.53 us -> none  [on_device(): part = jnp.einsum('sab,bq->qsa', timed, mode2_factor, precision=HIGH)]
  transfers between devices with their start and end apart: 3 -> 0, of which waited for: 3 -> 0; matrix products, arithmetic and copies ran while one was open for 0% -> 0% of each run, Pallas kernels for 0% -> 0%
where the time goes in v1:
time: 81.6 us; the launch traced here: 81.4 us
  Pallas kernels  77.9 us (95%)
  local copies, waits for them, and re-layouts  3.5 us (4%)
    pallas_call x1, Pallas kernels, on_device(): pl.pallas_call(kernel, out_shape=jax.ShapeDtypeStruct((ROWS // 16, 2, 8,...  77.9 us
    unnamed x3, local copies, waits for them, and re-layouts  2.73 us

profile of v1, /device:TPU:1, one launch (start us, length us, event | category | flops | bytes accessed | tf_op | source)
XLA Modules:
  0.0 81.4 jit_solution(1796698909441332917)
XLA Ops:
  0.0 0.8 copy.6.m3_hbm
  0.8 0.9 %copy.5.m2_hbm = f32[256,64]{1,0:T(8,128)S(1)} copy(f32[256,64]{0,1:T(8,128)} %param.5) | data formatting | bytes 131072 | tf_op args[1]
  1.7 1.0 %copy.7.start_hbm = f32[512,64]{1,0:T(8,128)S(1)} copy(f32[512,64]{0,1:T(8,128)} %param.7) | data formatting | bytes 262144 | tf_op args[3]
  2.7 77.9 %shard_map.46 = f32[32,2,8,64]{3,2,1,0:T(8,128)S(1)} custom-call(f32[32,512,256]{2,1,0:T(8,128)} %field_hbm.1, f32[256,64]{1,0:T(8,128)S(1)} %copy.5.m2_hbm, f32[32,16]{1,0:T(8,128)S(1)} %copy.6.m3_hbm, f32[512,64]{1,0:T(8,128)S(1)} %copy.7.start_hbm), custom_call_target="tpu_custom_call" | custom-call | tf_op jit(solution)/shard_map/pallas_call | solution.py:263
  80.6 0.8 copy.8

commit v2 on v1

v2 whole, which is shorter than its diff:
```python
import jax
import jax.numpy as jnp
from jax import lax
from jax.experimental import pallas as pl
from jax.experimental.pallas import tpu as pltpu
from jax.sharding import PartitionSpec as P

MESH = pl.DeviceIdType.MESH
HIGH = lax.Precision.HIGHEST
F32 = jnp.float32
BF16 = jnp.bfloat16

T3 = 32
R3 = 16
RANK = 64
ROWS = 512
COLS = 256
GX = 8
GY = 16
CHUNKS = 8
HALF = ROWS // CHUNKS // 2
RING = CHUNKS
LAG = 3
EARLY = 2
STEP = 4
ROUNDS = 4
SIDE = 4
PACKED = ROWS // 2
SHARE = 128 // GY
NN = (((1,), (0,)), ((), ()))
NT = (((1,), (1,)), ((), ()))


def dot(a, b, dims=NN):
    return lax.dot_general(a, b, dims, precision=HIGH, preferred_element_type=F32)


def bdot(a, b):
    return lax.dot_general(a, b, NN, preferred_element_type=F32)


def split(a):
    high = a.astype(BF16)
    return high, (a - high.astype(F32)).astype(BF16)


def swap(a):
    return pltpu.roll(a, 64, 1)


def lower_lanes(shape):
    return lax.broadcasted_iota(jnp.int32, shape, 1) < 64


def fold(m):
    return m[:64] + swap(m[64:])


def pair_up(s):
    return jnp.where(lower_lanes((32, 128)), s[:32], swap(s[32:]))


def unpair(p):
    return jnp.concatenate([p, swap(p)], axis=0)


def twice(s):
    low = lower_lanes((64, 128))
    zero = jnp.zeros_like(s)
    return jnp.concatenate([jnp.where(low, s, zero), jnp.where(low, zero, swap(s))], axis=0)


def inverse_factor(gram):
    lane = lax.broadcasted_iota(jnp.int32, (8, 128), 1)
    row = lax.broadcasted_iota(jnp.int32, (8, 128), 0)
    tiles = []
    for b in range(8):
        unit = jnp.where(lane == row + (64 + 8 * b), 1.0, 0.0)
        tiles.append(jnp.where(lane < 64, gram[8 * b : 8 * b + 8], unit))
    wide = lambda a: jnp.broadcast_to(a, (8, 128))
    for k in range(0, 64, STEP):
        own, at = divmod(k, 8)
        lines = [wide(tiles[own][at + j : at + j + 1]) for j in range(STEP)]
        cols = [[wide(t[:, k + j : k + j + 1]) for t in tiles[own:]] for j in range(STEP)]
        entry = [[wide(cols[j][0][at + n : at + n + 1]) if n >= j else None for n in range(STEP)] for j in range(STEP)]
        for j in range(STEP):
            inverse = 1.0 / entry[j][j]
            for n in range(j + 1, STEP):
                ratio = entry[j][n] * inverse
                for i in range(n, STEP):
                    entry[n][i] = entry[n][i] - ratio * entry[j][i]
                lines[n] = lines[n] - ratio * lines[j]
                cols[n] = [c - ratio * d for c, d in zip(cols[n], cols[j])]
            scaled = lines[j] * inverse
            for b in range(own, 8):
                col = cols[j][b - own]
                if b == own:
                    col = jnp.where(row > at + j, col, 0.0)
                tiles[b] = tiles[b] - col * scaled
    out = []
    for b in range(8):
        diag = jnp.sum(jnp.where(lane == row + 8 * b, tiles[b], 0.0), axis=1, keepdims=True)
        out.append(tiles[b] * lax.rsqrt(diag))
    return swap(jnp.concatenate(out, axis=0))


def kernel(
    field_hbm, m2_hbm, m3_hbm, start_hbm, out_ref,
    field, m2, m3, start,
    part, r1, r2, r3, pair, left_out, left_in, image, share_in, share, full,
    in_sem, small_sem, ring_send, ring_recv, ready, x_send, x_recv, s_send, s_recv, g_send, g_recv,
):
    mx = lax.axis_index("gx")
    my = lax.axis_index("gy")

    small = [
        pltpu.make_async_copy(src, dst, small_sem.at[n])
        for n, (src, dst) in enumerate(((m2_hbm, m2), (m3_hbm, m3), (start_hbm, start)))
    ]
    def load(c, h):
        at = pl.ds(pl.multiple_of(h * PACKED + c * HALF, HALF), HALF)
        return pltpu.make_async_copy(field_hbm.at[:, at, :], field.at[:, at, :], in_sem.at[c, h])

    small[0].start()
    small[1].start()
    for c in range(CHUNKS):
        for h in range(2):
            load(c, h).start()
    small[2].start()

    barrier = pltpu.get_barrier_semaphore()

    px, py = my // SIDE, lax.rem(my, SIDE)
    near_all = [{"gy": lax.rem(px + d, SIDE) * SIDE + py} for d in (1, 3)]
    near_all += [{"gy": px * SIDE + lax.rem(py + d, SIDE)} for d in (1, 3)]
    near_all += [{"gx": lax.rem(mx + d, GX)} for d in (2, 6)]
    near_all += [{"gx": mx + 1 - 2 * lax.rem(mx, 2)}]

    def greet(n):
        for device in near_all:
            pl.semaphore_signal(
                barrier if n == 0 else ready.at[n - 1], inc=1, device_id=device, device_id_type=MESH
            )

    def met(n):
        pl.semaphore_wait(barrier if n == 0 else ready.at[n - 1], len(near_all))

    greet(0)

    small[0].wait()
    small[1].wait()
    m2h, m2l = split(jnp.transpose(m2[...]))
    right = jnp.concatenate([m2h, m2l], axis=1)
    tall = jnp.where(
        lax.broadcasted_iota(jnp.int32, (128, R3), 0) // 8 == lax.broadcasted_iota(jnp.int32, (128, R3), 1), 1.0, 0.0
    )
    wide = jnp.where(
        lax.broadcasted_iota(jnp.int32, (T3, 256), 0) == lax.broadcasted_iota(jnp.int32, (T3, 256), 1) // 8, 1.0, 0.0
    )
    spread = dot(dot(tall, m3[...]), wide)
    same = (
        lax.broadcasted_iota(jnp.int32, (128, 256), 0) % 8 == lax.broadcasted_iota(jnp.int32, (128, 256), 1) % 8
    )
    wh, wl = split(jnp.where(same, spread, 0.0))
    w2 = jnp.concatenate([wh, wl], axis=0)
    low = lower_lanes((256, 128))

    def project(i0):
        tile = field[:, pl.ds(i0, 8), :].reshape(T3 * 8, COLS)
        th, tl = split(tile)
        return bdot(th, right) + bdot(tl, right)

    def compute(c):
        pairs = []
        for h in range(2):
            load(c, h).wait()
        for n in range(HALF // 8):
            i0 = pl.multiple_of(c * HALF + n * 8, 8)
            a, b = project(i0), project(i0 + PACKED)
            pairs.append(jnp.where(low, a + swap(a), b + swap(b)))
        blocks = []
        for n in range(0, HALF // 8, 2):
            bh, bl = split(jnp.concatenate(pairs[n : n + 2], axis=1))
            two = bdot(w2, bh)
            res = two[:128] + two[128:] + bdot(wh, bl)
            blocks += [res[:, :128].reshape(R3, 8, 128), res[:, 128:].reshape(R3, 8, 128)]
        return blocks

    first, second = (px, py), (py, px)

    def near(half, phase, step):
        if (half + phase) % 2 == 0:
            return {"gy": lax.rem(px + step + SIDE, SIDE) * SIDE + py}
        return {"gy": px * SIDE + lax.rem(py + step + SIDE, SIDE)}

    def send(src, dst, stage, c, half, phase, step):
        pltpu.make_async_remote_copy(
            src, dst.at[c, half, (1 - step) // 2], ring_send.at[stage], ring_recv.at[stage, c],
            device_id=near(half, phase, step), device_id_type=MESH,
        ).start()

    def arrive(dst, stage, c):
        pltpu.make_async_copy(dst.at[c], dst.at[c], ring_recv.at[stage, c]).wait()

    def hop(at, step):
        return lax.rem(at + step + SIDE, SIDE)

    def stage1(c):
        for half in range(2):
            far = hop(first[half], 2)
            for step in (1, -1):
                send(part.at[c, half, far, pl.ds(1 - step, 2)], r1, 0, c, half, 0, step)

    def stage2(c):
        arrive(r1, 0, c)
        for half in range(2):
            for step in (1, -1):
                to = hop(first[half], step)
                at = pl.ds(1 - step, 2)
                part[c, half, to, at] = part[c, half, to, at] + r1[c, half, (1 - step) // 2]
                send(part.at[c, half, to], r2, 1, c, half, 0, step)

    def stage3(c):
        arrive(r2, 1, c)
        for half in range(2):
            me = first[half]
            part[c, half, me] = part[c, half, me] + r2[c, half, 0] + r2[c, half, 1]
            for step in range(1, SIDE):
                to = hop(second[half], step)
                pltpu.make_async_remote_copy(
                    part.at[c, half, me, to], r3.at[c, half, step - 1], ring_send.at[2], ring_recv.at[2, c],
                    device_id=near(half, 1, step), device_id_type=MESH,
                ).start()

    def stage4(c):
        arrive(r3, 2, c)
        for half in range(2):
            at = pl.ds(pl.multiple_of(c * HALF + half * 16, 16), 16)
            total = part[c, half, first[half], second[half]]
            for step in range(1, SIDE):
                total = total + r3[c, half, step - 1]
            pair[at] = total

    stages = (stage2, stage3, stage4)

    def fill(c):
        blocks = compute(c)
        for n in range(2):
            at = slice(8 * n, 8 * n + 8)
            part[c, 0, :, :, at] = blocks[n].reshape(SIDE, SIDE, 8, 128)
            square = blocks[2 + n].reshape(SIDE, SIDE, 8, 128)
            for k in range(SIDE):
                part[c, 1, :, k, at] = square[k]

    @pl.loop(0, EARLY)
    def _(c):
        fill(c)

    met(0)
    greet(1)

    @pl.loop(0, EARLY)
    def _(c):
        stage1(c)

    @pl.loop(EARLY, RING)
    def _(c):
        fill(c)
        stage1(c)
        for n in range(1, ROUNDS):
            @pl.when(c == EARLY + 2 * n - 1)
            def _(n=n):
                met(n)
                if n + 1 < ROUNDS:
                    greet(n + 1)

        for n, stage in enumerate(stages):
            @pl.when(c >= LAG * (n + 1))
            def _(n=n, stage=stage):
                stage(c - LAG * (n + 1))

    small[2].wait()
    basis = jnp.concatenate([start[:, :PACKED], start[:, PACKED:]], axis=0)

    @pl.loop(RING, RING + 3 * LAG)
    def _(c):
        for n, stage in enumerate(stages):
            at = c - LAG * (n + 1)

            @pl.when((at >= 0) & (at < RING))
            def _(at=at, stage=stage):
                stage(at)

    def sum_over_gx(n, rows, value):
        src = left_out.at[n, pl.ds(0, rows)]
        dst = left_in.at[n, :, pl.ds(0, rows)]
        src[...] = value

        @pl.loop(1, GX)
        def _(r):
            pltpu.make_async_remote_copy(
                src, left_in.at[n, r - 1, pl.ds(0, rows)], x_send.at[n], x_recv.at[n],
                device_id={"gx": lax.rem(mx + r, GX)}, device_id_type=MESH,
            ).start()

        pltpu.make_async_copy(dst, dst, x_recv.at[n]).wait()
        total = value
        for r in range(GX - 1):
            total = total + left_in[n, r, :rows]
        return total, lambda: pltpu.make_async_copy(dst, dst, x_send.at[n]).wait()

    def sum_over_gy(n, value, beside):
        image[n] = value

        @pl.loop(1, GY)
        def _(r):
            dest = lax.rem(my + r, GY)
            pltpu.make_async_remote_copy(
                image.at[n, pl.ds(pl.multiple_of(dest * SHARE, SHARE), SHARE)], share_in.at[n, r - 1],
                s_send.at[n], s_recv.at[n], device_id={"gy": dest}, device_id_type=MESH,
            ).start()

        pltpu.make_async_copy(share_in.at[n], share_in.at[n], s_recv.at[n]).wait()
        total = image[n, pl.ds(pl.multiple_of(my * SHARE, SHARE), SHARE)]
        for r in range(GY - 1):
            total = total + share_in[n, r]
        share[n] = total
        full[n, my] = total

        @pl.loop(1, GY)
        def _(r):
            pltpu.make_async_remote_copy(
                share.at[n], full.at[n, my], g_send.at[n], g_recv.at[n],
                device_id={"gy": lax.rem(my + r, GY)}, device_id_type=MESH,
            ).start()

        aside = beside()
        pltpu.make_async_copy(share_in.at[n], share_in.at[n], g_recv.at[n]).wait()

        def end():
            pltpu.make_async_copy(share_in.at[n], share_in.at[n], s_send.at[n]).wait()
            pltpu.make_async_copy(share_in.at[n], share_in.at[n], g_send.at[n]).wait()

        return full[n].reshape(128, PACKED), aside, end

    low64 = lower_lanes((64, 128))
    units = pair[...]
    total, end0 = sum_over_gx(0, 32, pair_up(fold(dot(basis, units))))
    image1, _, end1 = sum_over_gy(0, dot(twice(unpair(total)), units, NT), lambda: None)
    left = fold(dot(image1, units))
    gram = fold(dot(image1, image1, NT))
    total, end2 = sum_over_gx(1, 64, jnp.where(low64, left, swap(gram)))
    raw, factor, end3 = sum_over_gy(
        1, dot(twice(total), units, NT), lambda: inverse_factor(swap(total))
    )
    image2 = dot(twice(factor), raw)
    gram = fold(dot(image2, image2, NT))
    total, end4 = sum_over_gx(2, 32, pair_up(gram))
    factor = inverse_factor(unpair(total))
    final = dot(twice(factor), image2) * jnp.sqrt(F32(ROWS * GX))
    out_ref[:, :PACKED] = final[:64]
    out_ref[:, PACKED:] = final[64:]
    for n, ref in enumerate((r1, r2, r3)):
        pltpu.make_async_copy(ref, ref, ring_send.at[n]).wait()
    for end in (end0, end1, end2, end3, end4):
        end()


def on_device(field, mode2_factor, mode3_factor, start_factor):
    dma = pltpu.SemaphoreType.DMA
    out = pl.pallas_call(
        kernel,
        out_shape=jax.ShapeDtypeStruct((RANK, ROWS), F32),
        in_specs=[pl.BlockSpec(memory_space=pl.ANY)] * 4,
        out_specs=pl.BlockSpec(memory_space=pltpu.VMEM),
        scratch_shapes=[
            pltpu.VMEM((T3, ROWS, COLS), F32),
            pltpu.VMEM((RANK, COLS), F32),
            pltpu.VMEM((R3, T3), F32),
            pltpu.VMEM((RANK, ROWS), F32),
            pltpu.VMEM((RING, 2, SIDE, SIDE, 16, 128), F32),
            pltpu.VMEM((RING, 2, 2, 2, 16, 128), F32),
            pltpu.VMEM((RING, 2, 2, SIDE, 16, 128), F32),
            pltpu.VMEM((RING, 2, SIDE - 1, 16, 128), F32),
            pltpu.VMEM((PACKED, 128), F32),
            pltpu.VMEM((3, 64, 128), F32),
            pltpu.VMEM((3, GX - 1, 64, 128), F32),
            pltpu.VMEM((2, 128, PACKED), F32),
            pltpu.VMEM((2, GY - 1, SHARE, PACKED), F32),
            pltpu.VMEM((2, SHARE, PACKED), F32),
            pltpu.VMEM((2, GY, SHARE, PACKED), F32),
            dma((CHUNKS, 2)),
            dma((3,)),
            dma((3,)), dma((3, RING)),
            pltpu.SemaphoreType.REGULAR((ROUNDS - 1,)),
            dma((3,)), dma((3,)),
            dma((2,)), dma((2,)),
            dma((2,)), dma((2,)),
        ],
        compiler_params=pltpu.CompilerParams(
            collective_id=0, has_side_effects=True, vmem_limit_bytes=60 * 1024 * 1024
        ),
    )(field, mode2_factor.T, mode3_factor.T, start_factor.T)
    return out.T


def solution(mesh):
    placed = (P(None, "gx", "gy"), P("gy", None), P(), P("gx", None))
    return jax.shard_map(
        on_device, mesh=mesh, in_specs=placed, out_specs=P("gx", None), check_vma=False
    )
```

time: 81.6 us -> 73.5 us (0.901)
  Pallas kernels: 77.9 us -> 71.8 us
  local copies, waits for them, and re-layouts: 3.5 us -> 1.57 us
    pallas_call x1, Pallas kernels: 77.9 us -> 71.8 us  [on_device(): pl.pallas_call(kernel, out_shape=jax.ShapeDtypeStruct((RANK, ROWS), F32),...]
    unnamed x3 -> x1, local copies, waits for them, and re-layouts: 2.73 us -> 1.57 us
where the time goes in v2:
time: 73.5 us; the launch traced here: 73.4 us
  Pallas kernels  71.8 us (98%)
  local copies, waits for them, and re-layouts  1.57 us (2%)
    pallas_call x1, Pallas kernels, on_device(): pl.pallas_call(kernel, out_shape=jax.ShapeDtypeStruct((RANK, ROWS), F32),...  71.8 us
    unnamed x1, local copies, waits for them, and re-layouts  1.57 us

profile of v2, /device:TPU:1, one launch (start us, length us, event | category | flops | bytes accessed | tf_op | source)
XLA Modules:
  0.0 73.4 jit_solution(9079628709404873226)
XLA Ops:
  0.0 71.8 %shard_map.46 = f32[64,512]{1,0:T(8,128)} custom-call(f32[32,512,256]{2,1,0:T(8,128)} %field_hbm.1, f32[64,256]{1,0:T(8,128)} %bitcast.6, f32[16,32]{1,0:T(8,128)} %bitcast.7, f32[64,512]{1,0:T(8,128)} %bitcast.5), custom_call_target="tpu_custom_call" | custom-call | tf_op jit(solution)/shard_map/pallas_call | solution.py:371
  71.8 1.6 %copy.6 = f32[512,64]{0,1:T(8,128)} copy(f32[512,64]{0,1:T(8,128)} %bitcast.4) | data formatting | bytes 262144

commit v3 on v2

--- a/solution.py
+++ b/solution.py
@@ -1,3 +1,5 @@
+import functools
+
 import jax
 import jax.numpy as jnp
 from jax import lax
@@ -20,10 +22,11 @@
 CHUNKS = 8
 HALF = ROWS // CHUNKS // 2
 RING = CHUNKS
-LAG = 3
-EARLY = 2
-STEP = 4
-ROUNDS = 4
+LAG = 6
+EARLY = 3
+STEP = 8
+SECOND = 5
+THIRD = 11
 SIDE = 4
 PACKED = ROWS // 2
 SHARE = 128 // GY
@@ -107,8 +110,8 @@
 def kernel(
     field_hbm, m2_hbm, m3_hbm, start_hbm, out_ref,
     field, m2, m3, start,
-    part, r1, r2, r3, pair, left_out, left_in, image, share_in, share, full,
-    in_sem, small_sem, ring_send, ring_recv, ready, x_send, x_recv, s_send, s_recv, g_send, g_recv,
+    part, r1, r2, r3, pair, left_out, left_in, image, share_in, share, full, basis, lead, lead_in, lead_gx, lead_gy, lead_all,
+    lead_send, lead_recv, in_sem, small_sem, ring_send, ring_recv, x_send, x_recv, s_send, s_recv, g_send, g_recv,
 ):
     mx = lax.axis_index("gx")
     my = lax.axis_index("gy")
@@ -128,24 +131,16 @@
             load(c, h).start()
     small[2].start()
 
+    px, py = my // SIDE, lax.rem(my, SIDE)
     barrier = pltpu.get_barrier_semaphore()
 
-    px, py = my // SIDE, lax.rem(my, SIDE)
-    near_all = [{"gy": lax.rem(px + d, SIDE) * SIDE + py} for d in (1, 3)]
-    near_all += [{"gy": px * SIDE + lax.rem(py + d, SIDE)} for d in (1, 3)]
-    near_all += [{"gx": lax.rem(mx + d, GX)} for d in (2, 6)]
-    near_all += [{"gx": mx + 1 - 2 * lax.rem(mx, 2)}]
-
-    def greet(n):
-        for device in near_all:
-            pl.semaphore_signal(
-                barrier if n == 0 else ready.at[n - 1], inc=1, device_id=device, device_id_type=MESH
-            )
-
-    def met(n):
-        pl.semaphore_wait(barrier if n == 0 else ready.at[n - 1], len(near_all))
-
-    greet(0)
+    @pl.loop(1, GY)
+    def _(r):
+        pl.semaphore_signal(barrier, inc=1, device_id={"gy": lax.rem(my + r, GY)}, device_id_type=MESH)
+
+    @pl.loop(1, GX)
+    def _(r):
+        pl.semaphore_signal(barrier, inc=1, device_id={"gx": lax.rem(mx + r, GX)}, device_id_type=MESH)
 
     small[0].wait()
     small[1].wait()
@@ -164,6 +159,7 @@
     wh, wl = split(jnp.where(same, spread, 0.0))
     w2 = jnp.concatenate([wh, wl], axis=0)
     low = lower_lanes((256, 128))
+    low64 = lower_lanes((64, 128))
 
     def project(i0):
         tile = field[:, pl.ds(i0, 8), :].reshape(T3 * 8, COLS)
@@ -252,12 +248,72 @@
             for k in range(SIDE):
                 part[c, 1, :, k, at] = square[k]
 
+    small[2].wait()
+    for h in range(2):
+        for n, piece in enumerate(split(start[:, h * PACKED : h * PACKED + PACKED])):
+            basis[n, 64 * h : 64 * h + 64] = piece
+
+    def lead_part(k):
+        at = pl.ds(pl.multiple_of(k * 128, 128), 128)
+        bh, bl = basis[0, :, at], basis[1, :, at]
+        both = jnp.concatenate([bh, bl], axis=0)
+
+        def rows(x, y):
+            halves = [part[pl.ds(4 * k, 4), 0, x, y], part[pl.ds(4 * k, 4), 1, y, x]]
+            return jnp.stack(halves, axis=1).reshape(128, 128)
+
+        for s in range(R3 // 2):
+            x, y = divmod(s, SIDE)
+            uh, ul = split(jnp.concatenate([rows(x, y), rows(x + 2, y)], axis=1))
+            two = bdot(both, uh)
+            m = two[:128] + two[128:] + bdot(bh, ul)
+            value = jnp.where(low64, m[:64, :128] + swap(m[64:, :128]), m[64:, 128:] + swap(m[:64, 128:]))
+            value = value.reshape(8, 8, 128)
+            lead[:, s] = jnp.where(k == 0, value, lead[:, s] + value)
+
+    def lead_stage1():
+        @pl.loop(1, GX)
+        def _(r):
+            dest = lax.rem(mx + r, GX)
+            pltpu.make_async_remote_copy(
+                lead.at[dest], lead_in.at[r - 1], lead_send.at[0], lead_recv.at[0],
+                device_id={"gx": dest}, device_id_type=MESH,
+            ).start()
+
+    def lead_stage2():
+        pltpu.make_async_copy(lead_in, lead_in, lead_recv.at[0]).wait()
+        total = lead[mx]
+        for r in range(GX - 1):
+            total = total + lead_in[r]
+        lead_gx[...] = total
+
+        @pl.loop(1, GY)
+        def _(r):
+            dest = lax.rem(my + r, GY)
+            pltpu.make_async_remote_copy(
+                lead_gx.at[lax.rem(dest, 8)], lead_gy.at[r - 1], lead_send.at[1], lead_recv.at[1],
+                device_id={"gy": dest}, device_id_type=MESH,
+            ).start()
+
+    def lead_stage3():
+        pltpu.make_async_copy(lead_gy, lead_gy, lead_recv.at[1]).wait()
+        total = lead_gx[lax.rem(my, 8)]
+        for r in range(GY - 1):
+            total = total + lead_gy[r]
+        lead_all[mx] = jnp.where(my < 8, total, swap(total))
+
+        @pl.loop(1, GX)
+        def _(r):
+            pltpu.make_async_remote_copy(
+                lead_all.at[mx], lead_all.at[mx], lead_send.at[2], lead_recv.at[2],
+                device_id={"gx": lax.rem(mx + r, GX)}, device_id_type=MESH,
+            ).start()
+
     @pl.loop(0, EARLY)
     def _(c):
         fill(c)
 
-    met(0)
-    greet(1)
+    pl.semaphore_wait(barrier, GX + GY - 2)
 
     @pl.loop(0, EARLY)
     def _(c):
@@ -267,23 +323,28 @@
     def _(c):
         fill(c)
         stage1(c)
-        for n in range(1, ROUNDS):
-            @pl.when(c == EARLY + 2 * n - 1)
-            def _(n=n):
-                met(n)
-                if n + 1 < ROUNDS:
-                    greet(n + 1)
+
+        @pl.when(lax.rem(c, 4) == 3)
+        def _():
+            lead_part(c // 4)
 
         for n, stage in enumerate(stages):
             @pl.when(c >= LAG * (n + 1))
             def _(n=n, stage=stage):
                 stage(c - LAG * (n + 1))
 
-    small[2].wait()
-    basis = jnp.concatenate([start[:, :PACKED], start[:, PACKED:]], axis=0)
+    lead_stage1()
 
     @pl.loop(RING, RING + 3 * LAG)
     def _(c):
+        @pl.when(c == RING + SECOND)
+        def _():
+            lead_stage2()
+
+        @pl.when(c == RING + THIRD)
+        def _():
+            lead_stage3()
+
         for n, stage in enumerate(stages):
             at = c - LAG * (n + 1)
 
@@ -291,23 +352,24 @@
             def _(at=at, stage=stage):
                 stage(at)
 
-    def sum_over_gx(n, rows, value):
-        src = left_out.at[n, pl.ds(0, rows)]
-        dst = left_in.at[n, :, pl.ds(0, rows)]
-        src[...] = value
+    def sum_over_gx(n, value):
+        left_out[n] = value
 
         @pl.loop(1, GX)
         def _(r):
             pltpu.make_async_remote_copy(
-                src, left_in.at[n, r - 1, pl.ds(0, rows)], x_send.at[n], x_recv.at[n],
+                left_out.at[n], left_in.at[n, r - 1], x_send.at[n], x_recv.at[n],
                 device_id={"gx": lax.rem(mx + r, GX)}, device_id_type=MESH,
             ).start()
 
-        pltpu.make_async_copy(dst, dst, x_recv.at[n]).wait()
-        total = value
-        for r in range(GX - 1):
-            total = total + left_in[n, r, :rows]
-        return total, lambda: pltpu.make_async_copy(dst, dst, x_send.at[n]).wait()
+        def finish():
+            pltpu.make_async_copy(left_in.at[n], left_in.at[n], x_recv.at[n]).wait()
+            total = value
+            for r in range(GX - 1):
+                total = total + left_in[n, r]
+            return unpair(total)
+
+        return finish, lambda: pltpu.make_async_copy(left_in.at[n], left_in.at[n], x_send.at[n]).wait()
 
     def sum_over_gy(n, value, beside):
         image[n] = value
@@ -343,26 +405,32 @@
 
         return full[n].reshape(128, PACKED), aside, end
 
-    low64 = lower_lanes((64, 128))
-    units = pair[...]
-    total, end0 = sum_over_gx(0, 32, pair_up(fold(dot(basis, units))))
-    image1, _, end1 = sum_over_gy(0, dot(twice(unpair(total)), units, NT), lambda: None)
-    left = fold(dot(image1, units))
-    gram = fold(dot(image1, image1, NT))
-    total, end2 = sum_over_gx(1, 64, jnp.where(low64, left, swap(gram)))
+    uh, ul = split(pair[...])
+
+    def times_units(a, dims):
+        ah, al = split(a)
+        three = functools.partial(lax.dot_general, dimension_numbers=dims, preferred_element_type=F32)
+        two = three(jnp.concatenate([ah, al], axis=0), uh)
+        return two[:128] + two[128:] + three(ah, ul)
+
+    pltpu.make_async_copy(lead_all.at[pl.ds(0, 7)], lead_all.at[pl.ds(0, 7)], lead_recv.at[2]).wait()
+    image1, _, end1 = sum_over_gy(0, times_units(twice(lead_all[...].reshape(64, 128)), NT), lambda: None)
+    finish_left, end2 = sum_over_gx(0, pair_up(fold(times_units(image1, NN))))
+    finish_gram, end5 = sum_over_gx(2, pair_up(fold(dot(image1, image1, NT))))
     raw, factor, end3 = sum_over_gy(
-        1, dot(twice(total), units, NT), lambda: inverse_factor(swap(total))
+        1, times_units(twice(finish_left()), NT), lambda: inverse_factor(finish_gram())
     )
     image2 = dot(twice(factor), raw)
-    gram = fold(dot(image2, image2, NT))
-    total, end4 = sum_over_gx(2, 32, pair_up(gram))
-    factor = inverse_factor(unpair(total))
+    finish_gram, end4 = sum_over_gx(1, pair_up(fold(dot(image2, image2, NT))))
+    factor = inverse_factor(finish_gram())
     final = dot(twice(factor), image2) * jnp.sqrt(F32(ROWS * GX))
     out_ref[:, :PACKED] = final[:64]
     out_ref[:, PACKED:] = final[64:]
     for n, ref in enumerate((r1, r2, r3)):
         pltpu.make_async_copy(ref, ref, ring_send.at[n]).wait()
-    for end in (end0, end1, end2, end3, end4):
+    for n, ref in enumerate((lead_in, lead_gy, lead_all.at[pl.ds(0, 7)])):
+        pltpu.make_async_copy(ref, ref, lead_send.at[n]).wait()
+    for end in (end1, end2, end3, end4, end5):
         end()
 
 
@@ -383,16 +451,22 @@
             pltpu.VMEM((RING, 2, 2, SIDE, 16, 128), F32),
             pltpu.VMEM((RING, 2, SIDE - 1, 16, 128), F32),
             pltpu.VMEM((PACKED, 128), F32),
-            pltpu.VMEM((3, 64, 128), F32),
-            pltpu.VMEM((3, GX - 1, 64, 128), F32),
+            pltpu.VMEM((3, 32, 128), F32),
+            pltpu.VMEM((3, GX - 1, 32, 128), F32),
             pltpu.VMEM((2, 128, PACKED), F32),
             pltpu.VMEM((2, GY - 1, SHARE, PACKED), F32),
             pltpu.VMEM((2, SHARE, PACKED), F32),
             pltpu.VMEM((2, GY, SHARE, PACKED), F32),
+            pltpu.VMEM((2, 128, PACKED), BF16),
+            pltpu.VMEM((GX, 8, 8, 128), F32),
+            pltpu.VMEM((GX - 1, 8, 8, 128), F32),
+            pltpu.VMEM((8, 8, 128), F32),
+            pltpu.VMEM((GY - 1, 8, 128), F32),
+            pltpu.VMEM((GX, 8, 128), F32),
+            dma((3,)), dma((3,)),
             dma((CHUNKS, 2)),
             dma((3,)),
             dma((3,)), dma((3, RING)),
-            pltpu.SemaphoreType.REGULAR((ROUNDS - 1,)),
             dma((3,)), dma((3,)),
             dma((2,)), dma((2,)),
             dma((2,)), dma((2,)),

time: 73.5 us -> 70.2 us (0.955)
  Pallas kernels: 71.8 us -> 68.5 us
    pallas_call x1, Pallas kernels: 71.8 us -> 68.5 us  [on_device(): pl.pallas_call(kernel, out_shape=jax.ShapeDtypeStruct((RANK, ROWS), F32),...]
where the time goes in v3:
time: 70.2 us; the launch traced here: 70.1 us
  Pallas kernels  68.5 us (98%)
  local copies, waits for them, and re-layouts  1.57 us (2%)
    pallas_call x1, Pallas kernels, on_device(): pl.pallas_call(kernel, out_shape=jax.ShapeDtypeStruct((RANK, ROWS), F32),...  68.5 us
    unnamed x1, local copies, waits for them, and re-layouts  1.57 us

profile of v3, /device:TPU:1, one launch (start us, length us, event | category | flops | bytes accessed | tf_op | source)
XLA Modules:
  0.0 70.1 jit_solution(15595002496053549628)
XLA Ops:
  0.0 68.5 %shard_map.46 = f32[64,512]{1,0:T(8,128)} custom-call(f32[32,512,256]{2,1,0:T(8,128)} %field_hbm.1, f32[64,256]{1,0:T(8,128)} %bitcast.6, f32[16,32]{1,0:T(8,128)} %bitcast.7, f32[64,512]{1,0:T(8,128)} %bitcast.5), custom_call_target="tpu_custom_call" | custom-call | tf_op jit(solution)/shard_map/pallas_call | solution.py:439
  68.5 1.6 %copy.6 = f32[512,64]{0,1:T(8,128)} copy(f32[512,64]{0,1:T(8,128)} %bitcast.4) | data formatting | bytes 262144

commit v4 on v3

--- a/solution.py
+++ b/solution.py
@@ -22,11 +22,11 @@
 CHUNKS = 8
 HALF = ROWS // CHUNKS // 2
 RING = CHUNKS
-LAG = 6
+LAG = 8
 EARLY = 3
 STEP = 8
-SECOND = 5
-THIRD = 11
+SECOND = 6
+THIRD = 14
 SIDE = 4
 PACKED = ROWS // 2
 SHARE = 128 // GY
@@ -152,11 +152,13 @@
     wide = jnp.where(
         lax.broadcasted_iota(jnp.int32, (T3, 256), 0) == lax.broadcasted_iota(jnp.int32, (T3, 256), 1) // 8, 1.0, 0.0
     )
-    spread = dot(dot(tall, m3[...]), wide)
     same = (
         lax.broadcasted_iota(jnp.int32, (128, 256), 0) % 8 == lax.broadcasted_iota(jnp.int32, (128, 256), 1) % 8
     )
-    wh, wl = split(jnp.where(same, spread, 0.0))
+    wh, wl = (
+        jnp.where(same, bdot(bdot(tall.astype(BF16), piece).astype(BF16), wide.astype(BF16)), 0.0).astype(BF16)
+        for piece in split(m3[...])
+    )
     w2 = jnp.concatenate([wh, wl], axis=0)
     low = lower_lanes((256, 128))
     low64 = lower_lanes((64, 128))
@@ -248,19 +250,12 @@
             for k in range(SIDE):
                 part[c, 1, :, k, at] = square[k]
 
-    small[2].wait()
-    for h in range(2):
-        for n, piece in enumerate(split(start[:, h * PACKED : h * PACKED + PACKED])):
-            basis[n, 64 * h : 64 * h + 64] = piece
-
-    def lead_part(k):
-        at = pl.ds(pl.multiple_of(k * 128, 128), 128)
-        bh, bl = basis[0, :, at], basis[1, :, at]
+    def lead_part():
+        bh, bl = basis[0], basis[1]
         both = jnp.concatenate([bh, bl], axis=0)
 
         def rows(x, y):
-            halves = [part[pl.ds(4 * k, 4), 0, x, y], part[pl.ds(4 * k, 4), 1, y, x]]
-            return jnp.stack(halves, axis=1).reshape(128, 128)
+            return jnp.stack([part[:, 0, x, y], part[:, 1, y, x]], axis=1).reshape(PACKED, 128)
 
         for s in range(R3 // 2):
             x, y = divmod(s, SIDE)
@@ -269,7 +264,7 @@
             m = two[:128] + two[128:] + bdot(bh, ul)
             value = jnp.where(low64, m[:64, :128] + swap(m[64:, :128]), m[64:, 128:] + swap(m[:64, 128:]))
             value = value.reshape(8, 8, 128)
-            lead[:, s] = jnp.where(k == 0, value, lead[:, s] + value)
+            lead[:, s] = value
 
     def lead_stage1():
         @pl.loop(1, GX)
@@ -313,6 +308,11 @@
     def _(c):
         fill(c)
 
+    small[2].wait()
+    for h in range(2):
+        for n, piece in enumerate(split(start[:, h * PACKED : h * PACKED + PACKED])):
+            basis[n, 64 * h : 64 * h + 64] = piece
+
     pl.semaphore_wait(barrier, GX + GY - 2)
 
     @pl.loop(0, EARLY)
@@ -324,15 +324,12 @@
         fill(c)
         stage1(c)
 
-        @pl.when(lax.rem(c, 4) == 3)
-        def _():
-            lead_part(c // 4)
-
         for n, stage in enumerate(stages):
             @pl.when(c >= LAG * (n + 1))
             def _(n=n, stage=stage):
                 stage(c - LAG * (n + 1))
 
+    lead_part()
     lead_stage1()
 
     @pl.loop(RING, RING + 3 * LAG)

time: 70.2 us -> 69.2 us (0.986)
  Pallas kernels: 68.5 us -> 67.5 us
    pallas_call x1, Pallas kernels: 68.5 us -> 67.5 us  [on_device(): pl.pallas_call(kernel, out_shape=jax.ShapeDtypeStruct((RANK, ROWS), F32),...]
where the time goes in v4:
time: 69.2 us; the launch traced here: 69.1 us
  Pallas kernels  67.5 us (98%)
  local copies, waits for them, and re-layouts  1.57 us (2%)
    pallas_call x1, Pallas kernels, on_device(): pl.pallas_call(kernel, out_shape=jax.ShapeDtypeStruct((RANK, ROWS), F32),...  67.5 us
    unnamed x1, local copies, waits for them, and re-layouts  1.57 us

profile of v4, /device:TPU:1, one launch (start us, length us, event | category | flops | bytes accessed | tf_op | source)
XLA Modules:
  0.0 69.1 jit_solution(3597919901196515059)
XLA Ops:
  0.0 67.5 %shard_map.46 = f32[64,512]{1,0:T(8,128)} custom-call(f32[32,512,256]{2,1,0:T(8,128)} %field_hbm.1, f32[64,256]{1,0:T(8,128)} %bitcast.6, f32[16,32]{1,0:T(8,128)} %bitcast.7, f32[64,512]{1,0:T(8,128)} %bitcast.5), custom_call_target="tpu_custom_call" | custom-call | tf_op jit(solution)/shard_map/pallas_call | solution.py:436
  67.5 1.6 %copy.6 = f32[512,64]{0,1:T(8,128)} copy(f32[512,64]{0,1:T(8,128)} %bitcast.4) | data formatting | bytes 262144

commit v5 on v4

--- a/solution.py
+++ b/solution.py
@@ -134,11 +134,11 @@
     px, py = my // SIDE, lax.rem(my, SIDE)
     barrier = pltpu.get_barrier_semaphore()
 
-    @pl.loop(1, GY)
+    @pl.loop(1, GY, unroll=True)
     def _(r):
         pl.semaphore_signal(barrier, inc=1, device_id={"gy": lax.rem(my + r, GY)}, device_id_type=MESH)
 
-    @pl.loop(1, GX)
+    @pl.loop(1, GX, unroll=True)
     def _(r):
         pl.semaphore_signal(barrier, inc=1, device_id={"gx": lax.rem(mx + r, GX)}, device_id_type=MESH)
 
@@ -267,7 +267,7 @@
             lead[:, s] = value
 
     def lead_stage1():
-        @pl.loop(1, GX)
+        @pl.loop(1, GX, unroll=True)
         def _(r):
             dest = lax.rem(mx + r, GX)
             pltpu.make_async_remote_copy(
@@ -282,7 +282,7 @@
             total = total + lead_in[r]
         lead_gx[...] = total
 
-        @pl.loop(1, GY)
+        @pl.loop(1, GY, unroll=True)
         def _(r):
             dest = lax.rem(my + r, GY)
             pltpu.make_async_remote_copy(
@@ -297,7 +297,7 @@
             total = total + lead_gy[r]
         lead_all[mx] = jnp.where(my < 8, total, swap(total))
 
-        @pl.loop(1, GX)
+        @pl.loop(1, GX, unroll=True)
         def _(r):
             pltpu.make_async_remote_copy(
                 lead_all.at[mx], lead_all.at[mx], lead_send.at[2], lead_recv.at[2],
@@ -352,7 +352,7 @@
     def sum_over_gx(n, value):
         left_out[n] = value
 
-        @pl.loop(1, GX)
+        @pl.loop(1, GX, unroll=True)
         def _(r):
             pltpu.make_async_remote_copy(
                 left_out.at[n], left_in.at[n, r - 1], x_send.at[n], x_recv.at[n],
@@ -371,7 +371,7 @@
     def sum_over_gy(n, value, beside):
         image[n] = value
 
-        @pl.loop(1, GY)
+        @pl.loop(1, GY, unroll=True)
         def _(r):
             dest = lax.rem(my + r, GY)
             pltpu.make_async_remote_copy(
@@ -386,7 +386,7 @@
         share[n] = total
         full[n, my] = total
 
-        @pl.loop(1, GY)
+        @pl.loop(1, GY, unroll=True)
         def _(r):
             pltpu.make_async_remote_copy(
                 share.at[n], full.at[n, my], g_send.at[n], g_recv.at[n],

time: 69.2 us -> 69.1 us (level)
  no operation moved by 1% of the time
where the time goes in v5:
time: 69.1 us; the launch traced here: 68.9 us
  Pallas kernels  67.4 us (98%)
  local copies, waits for them, and re-layouts  1.57 us (2%)
    pallas_call x1, Pallas kernels, on_device(): pl.pallas_call(kernel, out_shape=jax.ShapeDtypeStruct((RANK, ROWS), F32),...  67.4 us
    unnamed x1, local copies, waits for them, and re-layouts  1.57 us

profile of v5, /device:TPU:1, one launch (start us, length us, event | category | flops | bytes accessed | tf_op | source)
XLA Modules:
  0.0 68.9 jit_solution(12960193275847458715)
XLA Ops:
  0.0 67.4 %shard_map.46 = f32[64,512]{1,0:T(8,128)} custom-call(f32[32,512,256]{2,1,0:T(8,128)} %field_hbm.1, f32[64,256]{1,0:T(8,128)} %bitcast.6, f32[16,32]{1,0:T(8,128)} %bitcast.7, f32[64,512]{1,0:T(8,128)} %bitcast.5), custom_call_target="tpu_custom_call" | custom-call | tf_op jit(solution)/shard_map/pallas_call | solution.py:436
  67.4 1.6 %copy.6 = f32[512,64]{0,1:T(8,128)} copy(f32[512,64]{0,1:T(8,128)} %bitcast.4) | data formatting | bytes 262144
